TPU v7x, 32 devices: a whole 2x2x4 slice. The times are simulated.
32 devices in a mesh: groups: 2 (over x), gx: 16 (over z, y, core).
Axes of the slice: x: 2, y: 2, z: 4, core: 2. Of those that a mesh axis runs over, the one named last changes fastest.
Arguments:
- fracture: float32 [2, 64, 4, 128], P(None, ('groups', 'gx')), parts along dimension 1, may hold values from -6 to 6
- cell_class: int32 [64, 4, 128], P(('groups', 'gx')), parts along dimension 0, may hold values from 0 to 1
- owner: int32 [64, 4, 128, 1], P(('groups', 'gx')), parts along dimension 0, may hold values from 0 to 15; in each aligned block of 1024 rows (0 to 1023, 1024 to 2047, ..., all dimensions but the last counted through in order) at most 80 rows name the same one
- matrix: float32 [128, 2, 40960], P(None, None, ('groups', 'gx')), parts along dimension 2, may hold values from -6 to 6
- velocity: float32 [2, 3], replicated, may hold values from -0.3 to 0.3
- coupling: float32 [2], replicated, may hold values from 0.2 to 0.6
- operators: float32 [2, 128, 128], replicated, may hold values from -1 to 1
Outputs:
- age_moments: float32 [2, 64, 4, 128], P(None, ('groups', 'gx')), parts along dimension 1
- matrix_moments: float32 [128, 2, 40960], P(None, None, ('groups', 'gx')), parts along dimension 2
There are 2 independent parts, one for each index of `groups`. A program takes and returns all parts, laid end to end along the dimension named above; an argument that names none is the same for every part. Nothing has to cross between parts.
Inputs may be any that keep to these rules, and one draw needn't show every extreme that they name: Among the cells of one index of gx, at most 80 have the same owner, and some owner takes exactly 80 of them.
All inputs are finite; a program needn't handle non-finite values.
Results may differ from a plain program's by a relative error of at most 0.0001.
Values sent between devices are 32-bit elements; how exact they have to be, the bound alone decides.
A program may use at most 64 MiB of HBM per device.

v0:
```python
import functools

import jax
import jax.numpy as jnp
from jax import lax
from jax.experimental import pallas as pl
from jax.experimental.pallas import tpu as pltpu
from jax.sharding import PartitionSpec as P

STEPS = 8
SUBSTEPS = 2
TIME_STEP = 0.125
MEAN_RATE = 2.0 * TIME_STEP
BLOCK = 4
LANES = 128
HALF = STEPS // 2

F32 = jnp.float32
BF16 = jnp.bfloat16
NN = (((1,), (0,)), ((), ()))
NT = (((1,), (1,)), ((), ()))


def full_dot(a, b, dims=NN):
    return lax.dot_general(a, b, dims, precision=lax.Precision.HIGHEST, preferred_element_type=F32)


def half_dot(a, b, dims=NN):
    return lax.dot_general(a, b, dims, preferred_element_type=F32)


def two_parts(x):
    high = x.astype(BF16)
    low = (x - high.astype(F32)).astype(BF16)
    return high, low


def iota(shape, dim):
    return lax.broadcasted_iota(jnp.int32, shape, dim)


def roll_rows(x, shift):
    return pltpu.roll(x, shift, x.ndim - 2)


def roll_lanes(x, shift):
    shift = shift % LANES
    return x if shift == 0 else pltpu.roll(x, shift, x.ndim - 1)


def kernel(
    n,
    cap,
    kinds,
    chunks,
    frac,
    cls,
    own,
    mat,
    vel,
    coup,
    ops,
    age_out,
    mat_out,
    hot,
    mat_v,
    s_hi,
    s_lo,
    main,
    rows_pow,
    cols_pow,
    cols_t,
    fields,
    cls_send,
    cls_recv,
    tile_send,
    tile_recv,
    h0_send,
    h0_recv,
    h1_send,
    h1_recv,
    h2_send,
    h2_recv,
    mat_sem,
    a_send_sem,
    a_recv_sem,
    h_send_sem,
    h_recv_sem,
):
    me = lax.axis_index("gx")
    row8 = iota((8, LANES), 0)
    lane8 = iota((8, LANES), 1)

    load = pltpu.make_async_copy(mat, mat_v, mat_sem)
    load.start()

    sides = ((0, -1), (1, 1))
    for d in range(1, BLOCK + 1):
        for side, sign in sides:
            source = me + sign * d

            @pl.when((source < 0) | (source >= n))
            def _():
                h0_recv[side, d - 1] = jnp.zeros(h0_recv.shape[2:], F32)
                h2_recv[side, d - 1] = jnp.zeros(h2_recv.shape[2:], F32)
                if d < BLOCK:
                    h1_recv[side, d - 1] = jnp.zeros(h1_recv.shape[2:], F32)

    barrier = pltpu.get_barrier_semaphore()

    @pl.loop(1, n)
    def _(d):
        pl.semaphore_signal(
            barrier,
            inc=1,
            device_id={"gx": lax.rem(me + d, n)},
            device_id_type=pl.DeviceIdType.MESH,
        )

    def exchange(send, recv, which, d, peer, landing):
        return pltpu.make_async_remote_copy(
            src_ref=send.at[peer],
            dst_ref=recv.at[landing],
            send_sem=a_send_sem.at[which, d],
            recv_sem=a_recv_sem.at[which, landing],
            device_id={"gx": peer},
            device_id_type=pl.DeviceIdType.MESH,
        )

    def exchange_start(send, recv, which):
        @pl.loop(1, n)
        def _(d):
            exchange(send, recv, which, d, lax.rem(me + d, n), me).start()

        recv[me] = send[me]

    def exchange_arrived(send, recv, which):
        @pl.loop(1, n)
        def _(d):
            source = lax.rem(me + n - d, n)
            exchange(send, recv, which, d, source, source).wait_recv()

    def exchange_sent(send, recv, which):
        @pl.loop(1, n)
        def _(d):
            exchange(send, recv, which, d, lax.rem(me + d, n), me).wait_send()

    def halo(send, recv, which, d, side, sign, rows):
        return pltpu.make_async_remote_copy(
            src_ref=send.at[pl.ds(0, rows)],
            dst_ref=recv.at[side, d - 1, pl.ds(0, rows)],
            send_sem=h_send_sem.at[which, side, d - 1],
            recv_sem=h_recv_sem.at[which, side, d - 1],
            device_id={"gx": me - sign * d},
            device_id_type=pl.DeviceIdType.MESH,
        )

    def halo_each(send, recv, which, reach, rows_of, what):
        for d in range(1, reach + 1):
            for side, sign in sides:
                peer = me + sign * d if what == "arrived" else me - sign * d

                @pl.when((peer >= 0) & (peer < n))
                def _():
                    copy = halo(send, recv, which, d, side, sign, rows_of(d))
                    if what == "start":
                        copy.start()
                    elif what == "arrived":
                        copy.wait_recv()
                    else:
                        copy.wait_send()

    owner_f = own[...].astype(F32)
    class_f = cls[...].astype(F32)
    owner_row = iota((n, LANES), 0).astype(F32)
    named = [jnp.where(owner_row == owner_f[r : r + 1, :], 1.0, 0.0) for r in range(8)]
    named_all = jnp.concatenate(named, axis=0).astype(BF16)
    earlier = jnp.where(iota((LANES, LANES), 0) < iota((LANES, LANES), 1), 1.0, 0.0).astype(BF16)
    before = half_dot(named_all, earlier)
    total = half_dot(named_all, jnp.ones((LANES, LANES), BF16))
    base = jnp.zeros((n, LANES), F32)
    places = []
    for r in range(8):
        count = before[r * n : (r + 1) * n] + base
        base = base + total[r * n : (r + 1) * n]
        arrival = jnp.sum(named[r] * count, axis=0, keepdims=True)
        places.append(owner_f[r : r + 1, :] * float(LANES) + arrival)
    slot_row = iota((LANES, LANES), 0).astype(F32)

    @pl.loop(0, n)
    def _(e):
        start = pl.multiple_of(e * LANES, LANES)
        shift = (e * LANES).astype(F32)
        for r in range(8):
            hit = slot_row == (places[r] - shift)
            hot[pl.ds(start, LANES), r * LANES : (r + 1) * LANES] = jnp.where(hit, 1.0, 0.0).astype(
                BF16
            )

    class_rows = jnp.concatenate(
        [jnp.broadcast_to(class_f[r : r + 1, :], (16, LANES)) for r in range(8)], axis=1
    ).astype(BF16)
    class_out = half_dot(class_rows, hot[...], NT)
    for e in range(n):
        cls_send[e] = class_out[0:1, e * LANES : (e + 1) * LANES]
    h0_send[0] = frac[0]
    h0_send[1] = frac[1]
    h0_send[2] = class_f

    pl.semaphore_wait(barrier, n - 1)
    exchange_start(cls_send, cls_recv, 0)
    halo_each(h0_send, h0_recv, 0, BLOCK, lambda d: 3, "start")

    rows_pow[...] = jnp.zeros(rows_pow.shape, F32)
    squares, fourths = [], []
    for k in range(kinds):
        first = ops[k]
        square = full_dot(first, first)
        fourth = full_dot(square, square)
        squares.append(square)
        fourths.append(fourth)
        at = k * STEPS
        rows_pow[at : at + 1] = first[0:1]
        rows_pow[at + 1 : at + 2] = square[0:1]
        rows_pow[at + 2 : at + 4] = full_dot(rows_pow[at : at + 8], square)[0:2]
        rows_pow[at + 4 : at + 8] = full_dot(rows_pow[at : at + 8], fourth)[0:4]

    load.wait()
    stride = 2 * chunks
    for m in range(2):
        for c in range(chunks):
            at = (m * chunks + c) * LANES
            block = mat_v[pl.ds(c * 2 + m, LANES, stride=stride), :]
            high, low = two_parts(block)
            s_hi[:, at : at + LANES] = high
            s_lo[:, at : at + LANES] = low

    powers = rows_pow[...]
    p_high, p_low = two_parts(powers)
    wide = half_dot(jnp.concatenate([p_high, p_low], axis=0), s_hi[...])
    count = kinds * STEPS
    q_all = wide[:count] + wide[count:] + half_dot(p_high, s_lo[...])

    exchange_arrived(cls_send, cls_recv, 0)
    rolled_lane = lane8

    def to_columns(blocks):
        out = [jnp.zeros((8, LANES), F32) for _ in range(chunks)]
        for s in range(n):
            at, off = divmod(s * cap, LANES)
            turned = roll_lanes(blocks[s], off)
            if off + cap <= LANES:
                out[at] = out[at] + turned
            else:
                out[at] = out[at] + jnp.where(rolled_lane >= off, turned, 0.0)
                out[at + 1] = out[at + 1] + jnp.where(rolled_lane < off, turned, 0.0)
        return out

    def from_columns(columns):
        out = []
        for s in range(n):
            at, off = divmod(s * cap, LANES)
            block = roll_lanes(columns[at], -off)
            if off + cap > LANES:
                block = jnp.where(
                    rolled_lane < LANES - off, block, roll_lanes(columns[at + 1], -off)
                )
            out.append(jnp.where(rolled_lane < cap, block, 0.0))
        return out

    column_class = to_columns([jnp.broadcast_to(cls_recv[s], (8, LANES)) for s in range(n)])

    steady0, steady1 = [], []
    for k in range(kinds):
        sums = jnp.sum(powers[k * STEPS : (k + 1) * STEPS], axis=1, keepdims=True)
        sums = jnp.broadcast_to(sums, (STEPS, LANES))
        zero_sum = jnp.zeros((STEPS, LANES), F32)
        one_sum = jnp.zeros((STEPS, LANES), F32)
        for i in range(STEPS):
            term = jnp.where(row8 >= i, sums[i : i + 1], 0.0)
            zero_sum = zero_sum + TIME_STEP * term
            one_sum = one_sum + (TIME_STEP * MEAN_RATE * i) * term
        steady0.append(zero_sum)
        steady1.append(one_sum)

    def pick(options, which):
        value = options[0]
        for k in range(1, kinds):
            value = jnp.where(which == float(k), options[k], value)
        return value

    step_row = (row8 + 1).astype(F32)
    tiles_a, tiles_b = [], []
    for c in range(chunks):
        parts = []
        for m in range(2):
            at = (m * chunks + c) * LANES
            parts.append(
                pick(
                    [q_all[k * STEPS : (k + 1) * STEPS, at : at + LANES] for k in range(kinds)],
                    column_class[c],
                )
            )
        free0 = parts[0] + pick(steady0, column_class[c])
        free1 = parts[1] + MEAN_RATE * step_row * parts[0] + pick(steady1, column_class[c])
        tiles_a.append(jnp.where(row8 < HALF, free0, roll_rows(free1, HALF)))
        tiles_b.append(jnp.where(row8 < HALF, roll_rows(free0, HALF), free1))
    for half, tiles in ((0, tiles_a), (1, tiles_b)):
        blocks = from_columns(tiles)
        for e in range(n):
            tile_send[half, e] = blocks[e]
        exchange_start(tile_send.at[half], tile_recv.at[half], 1 + half)

    eights = [full_dot(fourths[k], fourths[k]) for k in range(kinds)]
    e_high, e_low = two_parts(jnp.concatenate(eights, axis=0))
    nodes = eights[0].shape[0]
    for b in range(chunks):
        lanes = slice(b * 2 * LANES, (b + 1) * 2 * LANES)
        right = s_hi[:, lanes]
        both = half_dot(e_high, right) + half_dot(e_low, right) + half_dot(e_high, s_lo[:, lanes])
        for i in range(2):
            at = b * 2 + i
            which = column_class[at % chunks][0:1]
            main[:, at * LANES : (at + 1) * LANES] = pick(
                [
                    both[k * nodes : (k + 1) * nodes, i * LANES : (i + 1) * LANES]
                    for k in range(kinds)
                ],
                which,
            )

    wide_rows = kinds * 16
    cols_t[...] = jnp.zeros(cols_t.shape, F32)
    for k in range(kinds):
        turned = ops[k].T
        cols_pow[...] = jnp.zeros(cols_pow.shape, F32)
        cols_pow[0:1] = turned[0:1]
        cols_pow[1:2] = jnp.sum(turned, axis=0, keepdims=True)
        cols_pow[2:4] = full_dot(cols_pow[0:8], ops[k], NT)[0:2]
        cols_pow[4:8] = full_dot(cols_pow[0:8], squares[k], NT)[0:4]
        cols_pow[8:16] = full_dot(cols_pow[0:8], fourths[k], NT)
        zero_sum = jnp.zeros((1, LANES), F32)
        one_sum = jnp.zeros((1, LANES), F32)
        for i in range(STEPS):
            cols_t[k * 16 + 7 - i : k * 16 + 8 - i] = cols_pow[2 * i : 2 * i + 1]
            source_row = cols_pow[2 * i + 1 : 2 * i + 2]
            zero_sum = zero_sum + TIME_STEP * source_row
            one_sum = one_sum + (TIME_STEP * MEAN_RATE * i) * source_row
        cols_t[k * 16 + 8 : k * 16 + 9] = zero_sum
        cols_t[k * 16 + 9 : k * 16 + 10] = one_sum
    whole = cols_t[0:wide_rows]
    whole_high = whole.astype(BF16).astype(F32)
    cols_t[0:wide_rows] = whole_high
    cols_t[wide_rows : 2 * wide_rows] = whole_high
    cols_t[2 * wide_rows : 3 * wide_rows] = whole - whole_high
    response = cols_t[...].T.astype(BF16)

    halo_each(h0_send, h0_recv, 0, BLOCK, lambda d: 3, "arrived")

    def window(recv, index, own_value, reach):
        left = [recv[0, d - 1, index] for d in range(reach, 0, -1)]
        right = [recv[1, d - 1, index] for d in range(1, reach + 1)]
        return jnp.stack(left + [own_value] + right)

    width = 2 * BLOCK + 1
    classes = window(h0_recv, 2, class_f, BLOCK)
    lane = iota((width, 8, LANES), 2)
    row = iota((width, 8, LANES), 1)
    slab = iota((width, 8, LANES), 0) + (me - BLOCK)
    centre = jnp.ones((width, 8, LANES), F32)
    coef = []
    first_last = (
        ((slab == 0) & (row < 4), (slab == n - 1) & (row >= 4)),
        (row % 4 == 0, row % 4 == 3),
        (lane == 0, lane == LANES - 1),
    )
    for direction in range(3):
        speed = pick([vel[k, direction] for k in range(kinds)], classes)
        if kinds == 1:
            speed = jnp.full((width, 8, LANES), speed)
        forward = jnp.maximum(speed, 0.0)
        backward = jnp.minimum(speed, 0.0)
        centre = centre - (forward - backward)
        coef.append(
            (
                jnp.where(first_last[direction][0], 0.0, forward),
                jnp.where(first_last[direction][1], 0.0, -backward),
            )
        )
    kappa = pick([coup[k] for k in range(kinds)], classes)
    answers = []
    for i in range(STEPS):
        answers.append(
            kappa
            * pick([powers[k * STEPS + i : k * STEPS + i + 1, 0:1] for k in range(kinds)], classes)
        )

    upper_half = row >= 4

    def advect(u, keep_from, keep_to):
        span = keep_to - keep_from
        pad = jnp.zeros((1, 8, LANES), F32)
        out = []
        part = slice(keep_from, keep_to)
        for m in range(2):
            x = u[m]
            previous = jnp.concatenate([pad, x[: span - 1]], axis=0)
            following = jnp.concatenate([x[1:], pad], axis=0)
            top = upper_half[part]
            low_x = roll_rows(jnp.where(top, previous, x), 4)
            high_x = roll_rows(jnp.where(top, x, following), 4)
            new = centre[part] * x + coef[0][0][part] * low_x + coef[0][1][part] * high_x
            new = new + coef[1][0][part] * roll_rows(x, 1) + coef[1][1][part] * roll_rows(x, 7)
            new = new + coef[2][0][part] * roll_lanes(x, 1) + coef[2][1][part] * roll_lanes(x, -1)
            out.append(new)
        return out

    def response_of(history, lo, hi, now, part):
        first = jnp.zeros((hi - lo, 8, LANES), F32)
        second = jnp.zeros((hi - lo, 8, LANES), F32)
        for at, (start, v0, v1) in history:
            lag = now - at
            a = v0[lo - start : hi - start]
            b = v1[lo - start : hi - start]
            gain = answers[lag][part]
            first = first + gain * a
            second = second + gain * (b + (MEAN_RATE * lag) * a if lag else b)
        return first, second

    def advect_two(u, lo, hi):
        u = advect(u, lo, hi)
        u = advect(u, lo, hi)
        return [x[1:-1] for x in u]

    def block_steps(u, free):
        history = []
        lo, hi = 0, width
        mine = []
        for s in range(BLOCK):
            u = advect_two(u, lo, hi)
            lo, hi = lo + 1, hi - 1
            part = slice(lo, hi)
            v0 = u[0] + TIME_STEP
            v1 = u[1] + MEAN_RATE * u[0]
            history.append((s, (lo, v0, v1)))
            first, second = response_of(history, lo, hi, s, part)
            gain = kappa[part]
            mine.append((v0[BLOCK - lo], v1[BLOCK - lo]))
            u = [
                v0 + gain * (free[s][0] + first - v0),
                v1 + gain * (free[s][1] + second - v1),
            ]
        return u, mine

    def to_cells(half):
        exchange_arrived(tile_send.at[half], tile_recv.at[half], 1 + half)
        slots = jnp.concatenate([tile_recv[half, s] for s in range(n)], axis=1)
        high, low = two_parts(slots)
        cells = half_dot(jnp.concatenate([high, low], axis=0), hot[...])
        cells = cells[:8] + cells[8:]
        for r in range(8):
            fields[r * 8 : (r + 1) * 8] = cells[:, r * LANES : (r + 1) * LANES]
        return [
            (fields[pl.ds(t, 8, stride=8), :], fields[pl.ds(HALF + t, 8, stride=8), :])
            for t in range(HALF)
        ]

    def to_owners(half, mine):
        for t in range(HALF):
            fields[pl.ds(t, 8, stride=8), :] = mine[t][0]
            fields[pl.ds(HALF + t, 8, stride=8), :] = mine[t][1]
        cells = jnp.concatenate([fields[r * 8 : (r + 1) * 8] for r in range(8)], axis=1)
        high, low = two_parts(cells)
        slots = half_dot(jnp.concatenate([high, low], axis=0), hot[...], NT)
        slots = slots[:8] + slots[8:]
        for e in range(n):
            tile_send[2 + half, e] = slots[:, e * LANES : (e + 1) * LANES]
        exchange_start(tile_send.at[2 + half], tile_recv.at[2 + half], 3 + half)

    early = to_cells(0)
    for t in range(BLOCK - 1):
        h1_send[2 * t] = early[t][0]
        h1_send[2 * t + 1] = early[t][1]
    halo_each(h1_send, h1_recv, 1, BLOCK - 1, lambda d: 2 * (BLOCK - d), "start")
    late = to_cells(1)
    halo_each(h1_send, h1_recv, 1, BLOCK - 1, lambda d: 2 * (BLOCK - d), "arrived")
    moments = [window(h0_recv, m, frac[m], BLOCK) for m in range(2)]
    free = [
        [window(h1_recv, 2 * s + m, early[s][m], BLOCK - 1 - s) for m in range(2)]
        for s in range(BLOCK)
    ]
    moments, mine = block_steps(moments, free)

    own_part = slice(BLOCK, BLOCK + 1)
    h2_send[0] = moments[0][0]
    h2_send[1] = moments[1][0]
    late_free = []
    for t in range(HALF):
        past = [(s, (BLOCK, mine[s][0][None], mine[s][1][None])) for s in range(HALF)]
        first, second = response_of(past, BLOCK, BLOCK + 1, HALF + t, own_part)
        late_free.append((late[t][0] + first[0], late[t][1] + second[0]))
        if t < BLOCK - 1:
            h2_send[2 + 2 * t] = late_free[t][0]
            h2_send[3 + 2 * t] = late_free[t][1]
    halo_each(h2_send, h2_recv, 2, BLOCK, lambda d: 2 + 2 * (BLOCK - d), "start")
    to_owners(0, mine)
    halo_each(h2_send, h2_recv, 2, BLOCK, lambda d: 2 + 2 * (BLOCK - d), "arrived")
    moments = [window(h2_recv, m, moments[m][0], BLOCK) for m in range(2)]
    free = [
        [window(h2_recv, 2 + 2 * s + m, late_free[s][m], BLOCK - 1 - s) for m in range(2)]
        for s in range(BLOCK)
    ]
    moments, mine = block_steps(moments, free)
    to_owners(1, mine)
    age_out[0] = moments[0][0]
    age_out[1] = moments[1][0]

    exchange_arrived(tile_send.at[2], tile_recv.at[2], 3)
    exchange_arrived(tile_send.at[3], tile_recv.at[3], 4)
    first_values = to_columns([tile_recv[2, s] for s in range(n)])
    last_values = to_columns([tile_recv[3, s] for s in range(n)])
    remaining = MEAN_RATE * (STEPS - 1 - row8).astype(F32)
    for c in range(chunks):
        a, b = first_values[c], last_values[c]
        v0 = jnp.where(row8 < HALF, a, roll_rows(b, HALF))
        v1 = jnp.where(row8 < HALF, roll_rows(a, HALF), b)
        v1 = v1 + remaining * v0
        right = []
        for m, value in ((0, v0), (1, v1)):
            pieces = []
            for k in range(kinds):
                belongs = column_class[c] == float(k)
                pieces.append(jnp.where(belongs, coup[k] * value, 0.0))
                pieces.append(jnp.where(belongs & (row8 == m), 1.0, 0.0))
            high, low = two_parts(jnp.concatenate(pieces, axis=0))
            rest = jnp.zeros((LANES - 3 * wide_rows, LANES), BF16)
            right.append(jnp.concatenate([high, low, high, rest], axis=0))
        added = half_dot(response, jnp.concatenate(right, axis=1))
        own0 = main[:, c * LANES : (c + 1) * LANES]
        own1 = main[:, (chunks + c) * LANES : (chunks + c + 1) * LANES]
        mat_out[pl.ds(2 * c, nodes, stride=stride), :] = own0 + added[:, :LANES]
        mat_out[pl.ds(2 * c + 1, nodes, stride=stride), :] = (
            own1 + (STEPS * MEAN_RATE) * own0 + added[:, LANES:]
        )

    exchange_sent(cls_send, cls_recv, 0)
    for which in range(4):
        exchange_sent(tile_send.at[which], tile_recv.at[which], 1 + which)
    halo_each(h0_send, h0_recv, 0, BLOCK, lambda d: 3, "sent")
    halo_each(h1_send, h1_recv, 1, BLOCK - 1, lambda d: 2 * (BLOCK - d), "sent")
    halo_each(h2_send, h2_recv, 2, BLOCK, lambda d: 2 + 2 * (BLOCK - d), "sent")


def shards(fracture, cell_class, owner, matrix, velocity, coupling, operators):
    n = lax.axis_size("gx")
    nodes, _, slots = matrix.shape
    cap = slots // n
    kinds = operators.shape[0]
    chunks = slots // LANES
    flat = matrix.reshape(nodes, 2, chunks, LANES).transpose(0, 2, 1, 3)
    flat = flat.reshape(nodes * chunks * 2, LANES)
    vmem = pl.BlockSpec(memory_space=pltpu.VMEM)
    smem = pl.BlockSpec(memory_space=pltpu.SMEM)
    tall = 2 + 2 * (BLOCK - 1)
    age, out = pl.pallas_call(
        functools.partial(kernel, n, cap, kinds, chunks),
        out_shape=(
            jax.ShapeDtypeStruct((2, 8, LANES), F32),
            jax.ShapeDtypeStruct(flat.shape, F32),
        ),
        in_specs=[vmem, vmem, vmem, pl.BlockSpec(memory_space=pl.ANY), smem, smem, vmem],
        out_specs=(vmem, vmem),
        scratch_shapes=[
            pltpu.VMEM((n * LANES, 8 * LANES), BF16),
            pltpu.VMEM(flat.shape, F32),
            pltpu.VMEM((nodes, 2 * slots), BF16),
            pltpu.VMEM((nodes, 2 * slots), BF16),
            pltpu.VMEM((nodes, 2 * slots), F32),
            pltpu.VMEM((kinds * STEPS, nodes), F32),
            pltpu.VMEM((2 * STEPS, nodes), F32),
            pltpu.VMEM((LANES, nodes), F32),
            pltpu.VMEM((64, LANES), F32),
            pltpu.VMEM((n, 1, LANES), F32),
            pltpu.VMEM((n, 1, LANES), F32),
            pltpu.VMEM((4, n, 8, LANES), F32),
            pltpu.VMEM((4, n, 8, LANES), F32),
            pltpu.VMEM((3, 8, LANES), F32),
            pltpu.VMEM((2, BLOCK, 3, 8, LANES), F32),
            pltpu.VMEM((tall - 2, 8, LANES), F32),
            pltpu.VMEM((2, BLOCK - 1, tall - 2, 8, LANES), F32),
            pltpu.VMEM((tall, 8, LANES), F32),
            pltpu.VMEM((2, BLOCK, tall, 8, LANES), F32),
            pltpu.SemaphoreType.DMA,
            pltpu.SemaphoreType.DMA((5, n)),
            pltpu.SemaphoreType.DMA((5, n)),
            pltpu.SemaphoreType.DMA((3, 2, BLOCK)),
            pltpu.SemaphoreType.DMA((3, 2, BLOCK)),
        ],
        compiler_params=pltpu.CompilerParams(
            collective_id=0, has_side_effects=True, vmem_limit_bytes=48 * 1024 * 1024
        ),
        cost_estimate=pl.CostEstimate(
            flops=2 * 400 * nodes * 2 * slots, bytes_accessed=8 * 2 * nodes * slots, transcendentals=0
        ),
    )(
        fracture.reshape(2, 8, LANES),
        cell_class.reshape(8, LANES),
        owner.reshape(8, LANES),
        flat,
        velocity,
        coupling,
        operators,
    )
    out = out.reshape(nodes, chunks, 2, LANES).transpose(0, 2, 1, 3).reshape(matrix.shape)
    return age.reshape(fracture.shape), out


def solution(mesh):
    in_specs = (
        P(None, ("groups", "gx"), None, None),
        P(("groups", "gx"), None, None),
        P(("groups", "gx"), None, None, None),
        P(None, None, ("groups", "gx")),
        P(),
        P(),
        P(),
    )
    out_specs = (P(None, ("groups", "gx"), None, None), P(None, None, ("groups", "gx")))
    return jax.shard_map(shards, mesh=mesh, in_specs=in_specs, out_specs=out_specs, check_vma=False)
```

profile of v0, /device:TPU:0, one launch (start us, length us, event | category | flops | bytes accessed | tf_op | source)
XLA Modules:
  0.0 40.8 jit_solution(14374334223292051080)
XLA Ops:
  0.6 2.5 %copy.11 = f32[128,2,1280]{0,2,1:T(8,128)S(1)} copy(f32[128,2,1280]{2,1,0:T(2,128)} %param.10) | data formatting | bytes 2621440 | tf_op args[3]
  3.1 0.0 copy-start
  3.1 0.0 copy-start.1
  3.2 0.0 copy-start.2
  3.2 0.0 copy-start.3
  3.2 0.0 copy-start.4
  3.2 0.0 copy-start.5
  3.2 1.3 %copy.12 = f32[128,10,2,128]{3,2,1,0:T(2,128)S(1)} copy(f32[128,10,2,128]{0,3,1,2:T(8,128)S(1)} %bitcast.19) | data formatting | bytes 2621440 | tf_op jit(solution)/shard_map/transpose | solution.py:560
  4.5 0.0 copy-done
  4.5 0.0 copy-done.1
  4.5 0.0 copy-done.2
  4.5 0.0 copy-done.3
  4.5 0.0 copy-done.4
  4.6 0.0 copy-done.5
  4.6 32.3 %shard_map.86 = (f32[2,8,128]{2,1,0:T(8,128)S(1)}, f32[2560,128]{1,0:T(8,128)S(1)}) custom-call(f32[2,8,128]{2,1,0:T(8,128)S(1)} %bitcast.14, s32[8,128]{1,0:T(8,128)S(1)} %bitcast.16, s32[8,128]{1,0:T(8,128)S(1)} %bitcast.17, f32[2560,128]{1,0:T(8,128)S(1)} %bitcast.12, f32[2,3]{1,0:T(2,128)S(1)} %copy-done.4, f32[2]{0:T(128)S(1)} %copy-done.5, ...), custom_call_target="tpu_custom_call" | custom-call | flops 262144000 | bytes 2621440 | tf_op jit(solution)/shard_map/pallas_call | solution.py:565
  36.9 1.3 %copy.13 = f32[128,10,2,128]{0,3,1,2:T(8,128)S(1)} copy(f32[128,10,2,128]{3,2,1,0:T(2,128)S(1)} %bitcast.13) | data formatting | bytes 2621440 | tf_op jit(solution)/shard_map/reshape | solution.py:614
  38.2 2.0 %copy.14 = f32[128,2,1280]{2,1,0:T(2,128)} copy(f32[128,2,1280]{0,2,1:T(8,128)S(1)} %bitcast.18) | data formatting | bytes 2621440
  40.2 0.6 %copy.16 = f32[2,2,4,128]{3,2,1,0:T(4,128)} copy(f32[2,2,4,128]{3,2,1,0:T(4,128)S(1)} %bitcast.15) | data formatting | bytes 16384
Async XLA Ops:
  3.1 1.4 %copy-start = (f32[2,128,128]{2,1,0:T(8,128)S(1)}, f32[2,128,128]{2,1,0:T(8,128)}, u32[]{:S(2)}) copy-start(f32[2,128,128]{2,1,0:T(8,128)} %ops.1) | copy-start | bytes 393220
  3.1 1.4 %copy-start.1 = (f32[2,2,4,128]{3,2,1,0:T(4,128)S(1)}, f32[2,2,4,128]{3,2,1,0:T(4,128)}, u32[]{:S(2)}) copy-start(f32[2,2,4,128]{3,2,1,0:T(4,128)} %param.7) | copy-start | bytes 24580
  3.2 1.4 %copy-start.2 = (s32[2,4,128]{2,1,0:T(4,128)S(1)}, s32[2,4,128]{2,1,0:T(4,128)}, u32[]{:S(2)}) copy-start(s32[2,4,128]{2,1,0:T(4,128)} %param.8) | copy-start | bytes 12292
  3.2 1.4 %copy-start.3 = (s32[2,4,128,1]{2,3,1,0:T(1,128)S(1)}, s32[2,4,128,1]{2,3,1,0:T(1,128)}, u32[]{:S(2)}) copy-start(s32[2,4,128,1]{2,3,1,0:T(1,128)} %param.9) | copy-start | bytes 12292
  3.2 1.4 %copy-start.4 = (f32[2,3]{1,0:T(2,128)S(1)}, f32[2,3]{1,0:T(2,128)}, u32[]{:S(2)}) copy-start(f32[2,3]{1,0:T(2,128)} %vel.1) | copy-start | bytes 76
  3.2 1.4 %copy-start.5 = (f32[2]{0:T(128)S(1)}, f32[2]{0:T(128)}, u32[]{:S(2)}) copy-start(f32[2]{0:T(128)} %coup.1) | copy-start | bytes 28
where the time goes:
time: 40.9 us; the launch traced here: 40.8 us
  Pallas kernels  32.3 us (79%)
  local copies, waits for them, and re-layouts  7.73 us (19%)
  between operations  0.76 us (2%)
    pallas_call x1, Pallas kernels, shards(): pl.pallas_call(functools.partial(kernel, n, cap, kinds, chunks), out_shap...  32.3 us
    unnamed x15, local copies, waits for them, and re-layouts  5.15 us
    reshape x1, local copies, waits for them, and re-layouts, shards(): out.reshape(nodes, chunks, 2, LANES).transpose(0, 2, 1, 3)  1.29 us
    transpose x1, local copies, waits for them, and re-layouts, shards(): flat = matrix.reshape(nodes, 2, chunks, LANES).transpose(0, 2, 1, 3)  1.29 us

commit v1 on v0

--- a/solution.py
+++ b/solution.py
@@ -4,6 +4,7 @@
 import jax.numpy as jnp
 from jax import lax
 from jax.experimental import pallas as pl
+from jax.experimental.layout import Layout, with_layout_constraint
 from jax.experimental.pallas import tpu as pltpu
 from jax.sharding import PartitionSpec as P
 
@@ -63,6 +64,7 @@
     age_out,
     mat_out,
     hot,
+    hot_t,
     mat_v,
     s_hi,
     s_lo,
@@ -184,25 +186,47 @@
         count = before[r * n : (r + 1) * n] + base
         base = base + total[r * n : (r + 1) * n]
         arrival = jnp.sum(named[r] * count, axis=0, keepdims=True)
-        places.append(owner_f[r : r + 1, :] * float(LANES) + arrival)
-    slot_row = iota((LANES, LANES), 0).astype(F32)
-
-    @pl.loop(0, n)
-    def _(e):
-        start = pl.multiple_of(e * LANES, LANES)
-        shift = (e * LANES).astype(F32)
-        for r in range(8):
-            hit = slot_row == (places[r] - shift)
-            hot[pl.ds(start, LANES), r * LANES : (r + 1) * LANES] = jnp.where(hit, 1.0, 0.0).astype(
-                BF16
-            )
+        places.append(owner_f[r : r + 1, :] * float(cap) + arrival)
+    slot_lane = iota((LANES, LANES), 1).astype(F32)
+    for r in range(8):
+        place = jnp.broadcast_to(places[r], (LANES, LANES)).T
+        for c in range(chunks):
+            hit = slot_lane == (place - float(c * LANES))
+            hot_t[r * LANES : (r + 1) * LANES, c * LANES : (c + 1) * LANES] = jnp.where(
+                hit, 1.0, 0.0
+            ).astype(BF16)
+
+    def to_columns(blocks):
+        out = [jnp.zeros((8, LANES), F32) for _ in range(chunks)]
+        for s in range(n):
+            at, off = divmod(s * cap, LANES)
+            turned = roll_lanes(blocks[s], off)
+            if off + cap <= LANES:
+                out[at] = out[at] + turned
+            else:
+                out[at] = out[at] + jnp.where(lane8 >= off, turned, 0.0)
+                out[at + 1] = out[at + 1] + jnp.where(lane8 < off, turned, 0.0)
+        return out
+
+    def from_columns(columns):
+        out = []
+        for s in range(n):
+            at, off = divmod(s * cap, LANES)
+            block = roll_lanes(columns[at], -off)
+            if off + cap > LANES:
+                block = jnp.where(lane8 < LANES - off, block, roll_lanes(columns[at + 1], -off))
+            out.append(jnp.where(lane8 < cap, block, 0.0))
+        return out
+
+    def split_lanes(x):
+        return [x[:, c * LANES : (c + 1) * LANES] for c in range(chunks)]
 
     class_rows = jnp.concatenate(
         [jnp.broadcast_to(class_f[r : r + 1, :], (16, LANES)) for r in range(8)], axis=1
     ).astype(BF16)
-    class_out = half_dot(class_rows, hot[...], NT)
-    for e in range(n):
-        cls_send[e] = class_out[0:1, e * LANES : (e + 1) * LANES]
+    class_out = half_dot(class_rows, hot_t[...])
+    for e, block in enumerate(from_columns(split_lanes(class_out[:8]))):
+        cls_send[e] = block[0:1]
     h0_send[0] = frac[0]
     h0_send[1] = frac[1]
     h0_send[2] = class_f
@@ -210,6 +234,14 @@
     pl.semaphore_wait(barrier, n - 1)
     exchange_start(cls_send, cls_recv, 0)
     halo_each(h0_send, h0_recv, 0, BLOCK, lambda d: 3, "start")
+
+    slot_row = iota((LANES, LANES), 0).astype(F32)
+    for c in range(chunks):
+        for r in range(8):
+            hit = slot_row == (places[r] - float(c * LANES))
+            hot[c * LANES : (c + 1) * LANES, r * LANES : (r + 1) * LANES] = jnp.where(
+                hit, 1.0, 0.0
+            ).astype(BF16)
 
     rows_pow[...] = jnp.zeros(rows_pow.shape, F32)
     squares, fourths = [], []
@@ -242,31 +274,6 @@
     q_all = wide[:count] + wide[count:] + half_dot(p_high, s_lo[...])
 
     exchange_arrived(cls_send, cls_recv, 0)
-    rolled_lane = lane8
-
-    def to_columns(blocks):
-        out = [jnp.zeros((8, LANES), F32) for _ in range(chunks)]
-        for s in range(n):
-            at, off = divmod(s * cap, LANES)
-            turned = roll_lanes(blocks[s], off)
-            if off + cap <= LANES:
-                out[at] = out[at] + turned
-            else:
-                out[at] = out[at] + jnp.where(rolled_lane >= off, turned, 0.0)
-                out[at + 1] = out[at + 1] + jnp.where(rolled_lane < off, turned, 0.0)
-        return out
-
-    def from_columns(columns):
-        out = []
-        for s in range(n):
-            at, off = divmod(s * cap, LANES)
-            block = roll_lanes(columns[at], -off)
-            if off + cap > LANES:
-                block = jnp.where(
-                    rolled_lane < LANES - off, block, roll_lanes(columns[at + 1], -off)
-                )
-            out.append(jnp.where(rolled_lane < cap, block, 0.0))
-        return out
 
     column_class = to_columns([jnp.broadcast_to(cls_recv[s], (8, LANES)) for s in range(n)])
 
@@ -454,7 +461,7 @@
 
     def to_cells(half):
         exchange_arrived(tile_send.at[half], tile_recv.at[half], 1 + half)
-        slots = jnp.concatenate([tile_recv[half, s] for s in range(n)], axis=1)
+        slots = jnp.concatenate(to_columns([tile_recv[half, s] for s in range(n)]), axis=1)
         high, low = two_parts(slots)
         cells = half_dot(jnp.concatenate([high, low], axis=0), hot[...])
         cells = cells[:8] + cells[8:]
@@ -471,10 +478,9 @@
             fields[pl.ds(HALF + t, 8, stride=8), :] = mine[t][1]
         cells = jnp.concatenate([fields[r * 8 : (r + 1) * 8] for r in range(8)], axis=1)
         high, low = two_parts(cells)
-        slots = half_dot(jnp.concatenate([high, low], axis=0), hot[...], NT)
-        slots = slots[:8] + slots[8:]
-        for e in range(n):
-            tile_send[2 + half, e] = slots[:, e * LANES : (e + 1) * LANES]
+        slots = half_dot(jnp.concatenate([high, low], axis=0), hot_t[...])
+        for e, block in enumerate(from_columns(split_lanes(slots[:8] + slots[8:]))):
+            tile_send[2 + half, e] = block
         exchange_start(tile_send.at[2 + half], tile_recv.at[2 + half], 3 + half)
 
     early = to_cells(0)
@@ -557,7 +563,9 @@
     cap = slots // n
     kinds = operators.shape[0]
     chunks = slots // LANES
-    flat = matrix.reshape(nodes, 2, chunks, LANES).transpose(0, 2, 1, 3)
+    tiled = Layout((0, 2, 1, 3))
+    flat = with_layout_constraint(matrix.reshape(nodes, 2, chunks, LANES), tiled)
+    flat = flat.transpose(0, 2, 1, 3)
     flat = flat.reshape(nodes * chunks * 2, LANES)
     vmem = pl.BlockSpec(memory_space=pltpu.VMEM)
     smem = pl.BlockSpec(memory_space=pltpu.SMEM)
@@ -571,7 +579,8 @@
         in_specs=[vmem, vmem, vmem, pl.BlockSpec(memory_space=pl.ANY), smem, smem, vmem],
         out_specs=(vmem, vmem),
         scratch_shapes=[
-            pltpu.VMEM((n * LANES, 8 * LANES), BF16),
+            pltpu.VMEM((slots, 8 * LANES), BF16),
+            pltpu.VMEM((8 * LANES, slots), BF16),
             pltpu.VMEM(flat.shape, F32),
             pltpu.VMEM((nodes, 2 * slots), BF16),
             pltpu.VMEM((nodes, 2 * slots), BF16),
@@ -611,7 +620,8 @@
         coupling,
         operators,
     )
-    out = out.reshape(nodes, chunks, 2, LANES).transpose(0, 2, 1, 3).reshape(matrix.shape)
+    out = out.reshape(nodes, chunks, 2, LANES).transpose(0, 2, 1, 3)
+    out = with_layout_constraint(out, tiled).reshape(matrix.shape)
     return age.reshape(fracture.shape), out
 
 

time: 40.9 us -> 39 us (0.954)
  Pallas kernels: 32.3 us -> 30.8 us
  local copies, waits for them, and re-layouts: 7.73 us -> 7.27 us
    unnamed x15 -> x16, local copies, waits for them, and re-layouts: 5.15 us -> 7.27 us
    pallas_call x1, Pallas kernels: 32.3 us -> 30.8 us  [shards(): pl.pallas_call(functools.partial(kernel, n, cap, kinds, chunks), out_shap...]
    reshape x1 -> x0, local copies, waits for them, and re-layouts: 1.29 us -> none  [shards(): out.reshape(nodes, chunks, 2, LANES).transpose(0, 2, 1, 3)]
    transpose x1 -> x0, local copies, waits for them, and re-layouts: 1.29 us -> none  [shards(): flat = matrix.reshape(nodes, 2, chunks, LANES).transpose(0, 2, 1, 3)]
where the time goes in v1:
time: 39 us; the launch traced here: 38.7 us
  Pallas kernels  30.8 us (79%)
  local copies, waits for them, and re-layouts  7.27 us (19%)
  between operations  0.66 us (2%)
    pallas_call x1, Pallas kernels, shards(): pl.pallas_call(functools.partial(kernel, n, cap, kinds, chunks), out_shap...  30.8 us
    unnamed x16, local copies, waits for them, and re-layouts  7.27 us

profile of v1, /device:TPU:0, one launch (start us, length us, event | category | flops | bytes accessed | tf_op | source)
XLA Modules:
  0.0 38.7 jit_solution(1976348605308902129)
XLA Ops:
  0.6 0.0 copy-start
  0.6 1.3 %copy-done = f32[128,2,1280]{2,1,0:T(2,128)S(1)} copy-done((f32[128,2,1280]{2,1,0:T(2,128)S(1)}, f32[128,2,1280]{2,1,0:T(2,128)}, u32[]{:S(2)}) %copy-start) | copy-done | bytes 1310744
  1.9 0.0 copy-start.1
  2.0 0.9 %copy-done.1 = f32[2,128,128]{2,1,0:T(8,128)S(1)} copy-done((f32[2,128,128]{2,1,0:T(8,128)S(1)}, f32[2,128,128]{2,1,0:T(8,128)}, u32[]{:S(2)}) %copy-start.1) | copy-done | bytes 131096
  2.9 0.0 copy-start.2
  2.9 0.7 %copy-done.2 = f32[2,2,4,128]{3,2,1,0:T(4,128)S(1)} copy-done((f32[2,2,4,128]{3,2,1,0:T(4,128)S(1)}, f32[2,2,4,128]{3,2,1,0:T(4,128)}, u32[]{:S(2)}) %copy-start.2) | copy-done | bytes 8216
  3.6 0.0 copy-start.3
  3.6 0.7 %copy-done.3 = s32[2,4,128]{2,1,0:T(4,128)S(1)} copy-done((s32[2,4,128]{2,1,0:T(4,128)S(1)}, s32[2,4,128]{2,1,0:T(4,128)}, u32[]{:S(2)}) %copy-start.3) | copy-done | bytes 4120
  4.2 0.0 copy-start.4
  4.2 0.7 %copy-done.4 = s32[2,4,128,1]{2,3,1,0:T(1,128)S(1)} copy-done((s32[2,4,128,1]{2,3,1,0:T(1,128)S(1)}, s32[2,4,128,1]{2,3,1,0:T(1,128)}, u32[]{:S(2)}) %copy-start.4) | copy-done | bytes 4120
  4.9 0.0 copy-start.5
  4.9 0.7 %copy-done.5 = f32[2,3]{1,0:T(2,128)S(1)} copy-done((f32[2,3]{1,0:T(2,128)S(1)}, f32[2,3]{1,0:T(2,128)}, u32[]{:S(2)}) %copy-start.5) | copy-done | bytes 48
  5.6 0.0 copy-start.6
  5.6 0.7 %copy-done.6 = f32[2]{0:T(128)S(1)} copy-done((f32[2]{0:T(128)S(1)}, f32[2]{0:T(128)}, u32[]{:S(2)}) %copy-start.6) | copy-done | bytes 32
  6.3 30.8 %shard_map.86 = (f32[2,8,128]{2,1,0:T(8,128)S(1)}, f32[2560,128]{1,0:T(8,128)S(1)}) custom-call(f32[2,8,128]{2,1,0:T(8,128)S(1)} %bitcast.16, s32[8,128]{1,0:T(8,128)S(1)} %bitcast.18, s32[8,128]{1,0:T(8,128)S(1)} %bitcast.19, f32[2560,128]{1,0:T(8,128)S(1)} %bitcast.14, f32[2,3]{1,0:T(2,128)S(1)} %copy-done.5, f32[2]{0:T(128)S(1)} %copy-done.6, ...), custom_call_target="tpu_custom_call" | custom-call | flops 262144000 | bytes 2621440 | tf_op jit(solution)/shard_map/pallas_call | solution.py:573
  37.1 0.6 %copy.11 = f32[2,2,4,128]{3,2,1,0:T(4,128)} copy(f32[2,2,4,128]{3,2,1,0:T(4,128)S(1)} %bitcast.17) | data formatting | bytes 16384
  37.7 1.1 %copy.12 = f32[128,2,1280]{2,1,0:T(2,128)} copy(f32[128,2,1280]{2,1,0:T(2,128)S(1)} %bitcast.15) | data formatting | bytes 2621440
Async XLA Ops:
  0.6 1.3 %copy-start = (f32[128,2,1280]{2,1,0:T(2,128)S(1)}, f32[128,2,1280]{2,1,0:T(2,128)}, u32[]{:S(2)}) copy-start(f32[128,2,1280]{2,1,0:T(2,128)} %param.10) | copy-start | bytes 3932164
  1.9 0.9 %copy-start.1 = (f32[2,128,128]{2,1,0:T(8,128)S(1)}, f32[2,128,128]{2,1,0:T(8,128)}, u32[]{:S(2)}) copy-start(f32[2,128,128]{2,1,0:T(8,128)} %ops.1) | copy-start | bytes 393220
  2.9 0.7 %copy-start.2 = (f32[2,2,4,128]{3,2,1,0:T(4,128)S(1)}, f32[2,2,4,128]{3,2,1,0:T(4,128)}, u32[]{:S(2)}) copy-start(f32[2,2,4,128]{3,2,1,0:T(4,128)} %param.7) | copy-start | bytes 24580
  3.6 0.7 %copy-start.3 = (s32[2,4,128]{2,1,0:T(4,128)S(1)}, s32[2,4,128]{2,1,0:T(4,128)}, u32[]{:S(2)}) copy-start(s32[2,4,128]{2,1,0:T(4,128)} %param.8) | copy-start | bytes 12292
  4.2 0.7 %copy-start.4 = (s32[2,4,128,1]{2,3,1,0:T(1,128)S(1)}, s32[2,4,128,1]{2,3,1,0:T(1,128)}, u32[]{:S(2)}) copy-start(s32[2,4,128,1]{2,3,1,0:T(1,128)} %param.9) | copy-start | bytes 12292
  4.9 0.7 %copy-start.5 = (f32[2,3]{1,0:T(2,128)S(1)}, f32[2,3]{1,0:T(2,128)}, u32[]{:S(2)}) copy-start(f32[2,3]{1,0:T(2,128)} %vel.1) | copy-start | bytes 76
  5.6 0.7 %copy-start.6 = (f32[2]{0:T(128)S(1)}, f32[2]{0:T(128)}, u32[]{:S(2)}) copy-start(f32[2]{0:T(128)} %coup.1) | copy-start | bytes 28

commit v2 on v1

--- a/solution.py
+++ b/solution.py
@@ -14,6 +14,7 @@
 MEAN_RATE = 2.0 * TIME_STEP
 BLOCK = 4
 LANES = 128
+VMEM_BYTES = 63 * 1024 * 1024
 HALF = STEPS // 2
 
 F32 = jnp.float32
@@ -47,6 +48,89 @@
 def roll_lanes(x, shift):
     shift = shift % LANES
     return x if shift == 0 else pltpu.roll(x, shift, x.ndim - 1)
+
+
+def pick(options, which):
+    value = options[0]
+    for k in range(1, len(options)):
+        value = jnp.where(which == float(k), options[k], value)
+    return value
+
+
+def finish(
+    kinds,
+    chunks,
+    age_any,
+    main_any,
+    pack_any,
+    response_any,
+    coup_any,
+    age_out,
+    mat_out,
+    age_v,
+    main_v,
+    pack,
+    response_v,
+    coup,
+    added,
+    load_sem,
+    store_sem,
+):
+    nodes = response_any.shape[0]
+    stride = 2 * chunks
+    bands = 4
+    band = nodes // bands
+    rows = band * stride
+
+    def band_rows(i):
+        return pl.ds(i * rows, rows)
+
+    pairs = [(pack_any, pack), (response_any, response_v), (coup_any, coup), (age_any, age_v)]
+    pairs += [(main_any.at[band_rows(i)], main_v.at[band_rows(i)]) for i in range(bands)]
+    loads = [
+        pltpu.make_async_copy(source, target, load_sem.at[i])
+        for i, (source, target) in enumerate(pairs)
+    ]
+    for load in loads:
+        load.start()
+    for load in loads[:4]:
+        load.wait()
+    age_store = pltpu.make_async_copy(age_v, age_out, store_sem.at[bands])
+    age_store.start()
+    row8 = iota((8, LANES), 0)
+    wide_rows = kinds * 16
+    remaining = MEAN_RATE * (STEPS - 1 - row8).astype(F32)
+    rest = jnp.zeros((LANES - 3 * wide_rows, LANES), BF16)
+    right = []
+    for c in range(chunks):
+        a, b, which = pack[0, c], pack[1, c], pack[2, c]
+        v0 = jnp.where(row8 < HALF, a, roll_rows(b, HALF))
+        v1 = jnp.where(row8 < HALF, roll_rows(a, HALF), b)
+        v1 = v1 + remaining * v0
+        for m, value in ((0, v0), (1, v1)):
+            pieces = []
+            for k in range(kinds):
+                belongs = which == float(k)
+                pieces.append(jnp.where(belongs, coup[:, k : k + 1] * value, 0.0))
+                pieces.append(jnp.where(belongs & (row8 == m), 1.0, 0.0))
+            high, low = two_parts(jnp.concatenate(pieces, axis=0))
+            right.append(jnp.concatenate([high, low, high, rest], axis=0))
+    added[...] = half_dot(response_v[...].astype(BF16), jnp.concatenate(right, axis=1))
+    stores = []
+    for i in range(bands):
+        loads[4 + i].wait()
+        for at in range(stride):
+            where = pl.ds(i * rows + at, band, stride=stride)
+            more = added[i * band : (i + 1) * band, at * LANES : (at + 1) * LANES]
+            main_v[where, :] = main_v[where, :] + more
+        store = pltpu.make_async_copy(
+            main_v.at[band_rows(i)], mat_out.at[band_rows(i)], store_sem.at[i]
+        )
+        store.start()
+        stores.append(store)
+    for store in stores:
+        store.wait()
+    age_store.wait()
 
 
 def kernel(
@@ -54,15 +138,17 @@
     cap,
     kinds,
     chunks,
-    frac,
-    cls,
-    own,
+    frac_any,
+    cls_any,
+    own_any,
     mat,
-    vel,
-    coup,
-    ops,
+    vel_any,
+    coup_any,
+    ops_any,
     age_out,
-    mat_out,
+    main_any,
+    pack_out,
+    response_out,
     hot,
     hot_t,
     mat_v,
@@ -83,7 +169,14 @@
     h1_recv,
     h2_send,
     h2_recv,
-    mat_sem,
+    frac,
+    cls,
+    own,
+    vel,
+    coup,
+    ops,
+    load_sem,
+    store_sem,
     a_send_sem,
     a_recv_sem,
     h_send_sem,
@@ -93,8 +186,22 @@
     row8 = iota((8, LANES), 0)
     lane8 = iota((8, LANES), 1)
 
-    load = pltpu.make_async_copy(mat, mat_v, mat_sem)
-    load.start()
+    loads = [
+        pltpu.make_async_copy(source, target, load_sem.at[i])
+        for i, (source, target) in enumerate(
+            (
+                (own_any, own),
+                (cls_any, cls),
+                (frac_any, frac),
+                (ops_any, ops),
+                (mat, mat_v),
+                (vel_any, vel),
+                (coup_any, coup),
+            )
+        )
+    ]
+    for load in loads:
+        load.start()
 
     sides = ((0, -1), (1, 1))
     for d in range(1, BLOCK + 1):
@@ -172,6 +279,8 @@
                     else:
                         copy.wait_send()
 
+    loads[0].wait()
+    loads[1].wait()
     owner_f = own[...].astype(F32)
     class_f = cls[...].astype(F32)
     owner_row = iota((n, LANES), 0).astype(F32)
@@ -227,6 +336,7 @@
     class_out = half_dot(class_rows, hot_t[...])
     for e, block in enumerate(from_columns(split_lanes(class_out[:8]))):
         cls_send[e] = block[0:1]
+    loads[2].wait()
     h0_send[0] = frac[0]
     h0_send[1] = frac[1]
     h0_send[2] = class_f
@@ -243,6 +353,7 @@
                 hit, 1.0, 0.0
             ).astype(BF16)
 
+    loads[3].wait()
     rows_pow[...] = jnp.zeros(rows_pow.shape, F32)
     squares, fourths = [], []
     for k in range(kinds):
@@ -257,7 +368,8 @@
         rows_pow[at + 2 : at + 4] = full_dot(rows_pow[at : at + 8], square)[0:2]
         rows_pow[at + 4 : at + 8] = full_dot(rows_pow[at : at + 8], fourth)[0:4]
 
-    load.wait()
+    for load in loads[4:]:
+        load.wait()
     stride = 2 * chunks
     for m in range(2):
         for c in range(chunks):
@@ -289,12 +401,6 @@
             one_sum = one_sum + (TIME_STEP * MEAN_RATE * i) * term
         steady0.append(zero_sum)
         steady1.append(one_sum)
-
-    def pick(options, which):
-        value = options[0]
-        for k in range(1, kinds):
-            value = jnp.where(which == float(k), options[k], value)
-        return value
 
     step_row = (row8 + 1).astype(F32)
     tiles_a, tiles_b = [], []
@@ -327,14 +433,20 @@
         both = half_dot(e_high, right) + half_dot(e_low, right) + half_dot(e_high, s_lo[:, lanes])
         for i in range(2):
             at = b * 2 + i
-            which = column_class[at % chunks][0:1]
-            main[:, at * LANES : (at + 1) * LANES] = pick(
+            m, c = divmod(at, chunks)
+            value = pick(
                 [
                     both[k * nodes : (k + 1) * nodes, i * LANES : (i + 1) * LANES]
                     for k in range(kinds)
                 ],
-                which,
+                column_class[c][0:1],
             )
+            if m == 1:
+                mean = main[pl.ds(2 * c, nodes, stride=stride), :]
+                value = value + (STEPS * MEAN_RATE) * mean
+            main[pl.ds(2 * c + m, nodes, stride=stride), :] = value
+    store = pltpu.make_async_copy(main, main_any, store_sem)
+    store.start()
 
     wide_rows = kinds * 16
     cols_t[...] = jnp.zeros(cols_t.shape, F32)
@@ -360,7 +472,7 @@
     cols_t[0:wide_rows] = whole_high
     cols_t[wide_rows : 2 * wide_rows] = whole_high
     cols_t[2 * wide_rows : 3 * wide_rows] = whole - whole_high
-    response = cols_t[...].T.astype(BF16)
+    response_out[...] = cols_t[...].T
 
     halo_each(h0_send, h0_recv, 0, BLOCK, lambda d: 3, "arrived")
 
@@ -382,9 +494,11 @@
         (lane == 0, lane == LANES - 1),
     )
     for direction in range(3):
-        speed = pick([vel[k, direction] for k in range(kinds)], classes)
+        speed = pick(
+            [vel[k : k + 1, direction : direction + 1] for k in range(kinds)], classes
+        )
         if kinds == 1:
-            speed = jnp.full((width, 8, LANES), speed)
+            speed = jnp.broadcast_to(speed, (width, 8, LANES))
         forward = jnp.maximum(speed, 0.0)
         backward = jnp.minimum(speed, 0.0)
         centre = centre - (forward - backward)
@@ -394,7 +508,7 @@
                 jnp.where(first_last[direction][1], 0.0, -backward),
             )
         )
-    kappa = pick([coup[k] for k in range(kinds)], classes)
+    kappa = pick([coup[:, k : k + 1] for k in range(kinds)], classes)
     answers = []
     for i in range(STEPS):
         answers.append(
@@ -525,29 +639,11 @@
     exchange_arrived(tile_send.at[3], tile_recv.at[3], 4)
     first_values = to_columns([tile_recv[2, s] for s in range(n)])
     last_values = to_columns([tile_recv[3, s] for s in range(n)])
-    remaining = MEAN_RATE * (STEPS - 1 - row8).astype(F32)
     for c in range(chunks):
-        a, b = first_values[c], last_values[c]
-        v0 = jnp.where(row8 < HALF, a, roll_rows(b, HALF))
-        v1 = jnp.where(row8 < HALF, roll_rows(a, HALF), b)
-        v1 = v1 + remaining * v0
-        right = []
-        for m, value in ((0, v0), (1, v1)):
-            pieces = []
-            for k in range(kinds):
-                belongs = column_class[c] == float(k)
-                pieces.append(jnp.where(belongs, coup[k] * value, 0.0))
-                pieces.append(jnp.where(belongs & (row8 == m), 1.0, 0.0))
-            high, low = two_parts(jnp.concatenate(pieces, axis=0))
-            rest = jnp.zeros((LANES - 3 * wide_rows, LANES), BF16)
-            right.append(jnp.concatenate([high, low, high, rest], axis=0))
-        added = half_dot(response, jnp.concatenate(right, axis=1))
-        own0 = main[:, c * LANES : (c + 1) * LANES]
-        own1 = main[:, (chunks + c) * LANES : (chunks + c + 1) * LANES]
-        mat_out[pl.ds(2 * c, nodes, stride=stride), :] = own0 + added[:, :LANES]
-        mat_out[pl.ds(2 * c + 1, nodes, stride=stride), :] = (
-            own1 + (STEPS * MEAN_RATE) * own0 + added[:, LANES:]
-        )
+        pack_out[0, c] = first_values[c]
+        pack_out[1, c] = last_values[c]
+        pack_out[2, c] = column_class[c]
+    store.wait()
 
     exchange_sent(cls_send, cls_recv, 0)
     for which in range(4):
@@ -568,23 +664,26 @@
     flat = flat.transpose(0, 2, 1, 3)
     flat = flat.reshape(nodes * chunks * 2, LANES)
     vmem = pl.BlockSpec(memory_space=pltpu.VMEM)
-    smem = pl.BlockSpec(memory_space=pltpu.SMEM)
+    anywhere = pl.BlockSpec(memory_space=pl.ANY)
     tall = 2 + 2 * (BLOCK - 1)
-    age, out = pl.pallas_call(
+    coupling = coupling.reshape(1, kinds)
+    age, main, pack, response = pl.pallas_call(
         functools.partial(kernel, n, cap, kinds, chunks),
         out_shape=(
             jax.ShapeDtypeStruct((2, 8, LANES), F32),
             jax.ShapeDtypeStruct(flat.shape, F32),
+            jax.ShapeDtypeStruct((3, chunks, 8, LANES), F32),
+            jax.ShapeDtypeStruct((nodes, LANES), F32),
         ),
-        in_specs=[vmem, vmem, vmem, pl.BlockSpec(memory_space=pl.ANY), smem, smem, vmem],
-        out_specs=(vmem, vmem),
+        in_specs=[anywhere] * 7,
+        out_specs=(vmem, anywhere, vmem, vmem),
         scratch_shapes=[
             pltpu.VMEM((slots, 8 * LANES), BF16),
             pltpu.VMEM((8 * LANES, slots), BF16),
             pltpu.VMEM(flat.shape, F32),
             pltpu.VMEM((nodes, 2 * slots), BF16),
             pltpu.VMEM((nodes, 2 * slots), BF16),
-            pltpu.VMEM((nodes, 2 * slots), F32),
+            pltpu.VMEM(flat.shape, F32),
             pltpu.VMEM((kinds * STEPS, nodes), F32),
             pltpu.VMEM((2 * STEPS, nodes), F32),
             pltpu.VMEM((LANES, nodes), F32),
@@ -599,6 +698,13 @@
             pltpu.VMEM((2, BLOCK - 1, tall - 2, 8, LANES), F32),
             pltpu.VMEM((tall, 8, LANES), F32),
             pltpu.VMEM((2, BLOCK, tall, 8, LANES), F32),
+            pltpu.VMEM((2, 8, LANES), F32),
+            pltpu.VMEM((8, LANES), jnp.int32),
+            pltpu.VMEM((8, LANES), jnp.int32),
+            pltpu.VMEM(velocity.shape, F32),
+            pltpu.VMEM((1, kinds), F32),
+            pltpu.VMEM(operators.shape, F32),
+            pltpu.SemaphoreType.DMA((7,)),
             pltpu.SemaphoreType.DMA,
             pltpu.SemaphoreType.DMA((5, n)),
             pltpu.SemaphoreType.DMA((5, n)),
@@ -606,7 +712,7 @@
             pltpu.SemaphoreType.DMA((3, 2, BLOCK)),
         ],
         compiler_params=pltpu.CompilerParams(
-            collective_id=0, has_side_effects=True, vmem_limit_bytes=48 * 1024 * 1024
+            collective_id=0, has_side_effects=True, vmem_limit_bytes=VMEM_BYTES
         ),
         cost_estimate=pl.CostEstimate(
             flops=2 * 400 * nodes * 2 * slots, bytes_accessed=8 * 2 * nodes * slots, transcendentals=0
@@ -620,6 +726,26 @@
         coupling,
         operators,
     )
+    age, out = pl.pallas_call(
+        functools.partial(finish, kinds, chunks),
+        out_shape=(
+            jax.ShapeDtypeStruct((2, 8, LANES), F32),
+            jax.ShapeDtypeStruct(flat.shape, F32),
+        ),
+        in_specs=[anywhere] * 5,
+        out_specs=(anywhere, anywhere),
+        scratch_shapes=[
+            pltpu.VMEM((2, 8, LANES), F32),
+            pltpu.VMEM(flat.shape, F32),
+            pltpu.VMEM(pack.shape, F32),
+            pltpu.VMEM(response.shape, F32),
+            pltpu.VMEM((1, kinds), F32),
+            pltpu.VMEM((nodes, 2 * slots), F32),
+            pltpu.SemaphoreType.DMA((8,)),
+            pltpu.SemaphoreType.DMA((5,)),
+        ],
+        compiler_params=pltpu.CompilerParams(vmem_limit_bytes=VMEM_BYTES),
+    )(age, main, pack, response, coupling)
     out = out.reshape(nodes, chunks, 2, LANES).transpose(0, 2, 1, 3)
     out = with_layout_constraint(out, tiled).reshape(matrix.shape)
     return age.reshape(fracture.shape), out

time: 39 us -> 34.2 us (0.88)
  local copies, waits for them, and re-layouts: 7.27 us -> 0 us
  Pallas kernels: 30.8 us -> 33.4 us
    unnamed x16 -> x0, local copies, waits for them, and re-layouts: 7.27 us -> none
    pallas_call x0 -> x1, Pallas kernels: none -> 2.49 us  [shards(): pl.pallas_call(functools.partial(finish, kinds, chunks), out_shape=(jax.S...]
where the time goes in v2:
time: 34.2 us; the launch traced here: 34 us
  Pallas kernels  33.4 us (98%)
  between operations  0.64 us (2%)
    pallas_call x1, Pallas kernels, shards(): pl.pallas_call(functools.partial(kernel, n, cap, kinds, chunks), out_shap...  30.9 us
    pallas_call x1, Pallas kernels, shards(): pl.pallas_call(functools.partial(finish, kinds, chunks), out_shape=(jax.S...  2.49 us

profile of v2, /device:TPU:0, one launch (start us, length us, event | category | flops | bytes accessed | tf_op | source)
XLA Modules:
  0.0 34.0 jit_solution(18205433581406314768)
XLA Ops:
  0.6 30.9 %shard_map.86 = (f32[2,8,128]{2,1,0:T(8,128)}, f32[2560,128]{1,0:T(8,128)}, f32[3,10,8,128]{3,2,1,0:T(8,128)}, f32[128,128]{1,0:T(8,128)}) custom-call(f32[2,8,128]{2,1,0:T(8,128)} %bitcast.16, s32[8,128]{1,0:T(8,128)} %bitcast.17, s32[8,128]{1,0:T(8,128)} %bitcast.18, f32[2560,128]{1,0:T(8,128)} %bitcast.15, f32[2,3]{1,0:T(2,128)} %vel_any.1, ...), custom_call_target="tpu_custom_call" | custom-call | flops 262144000 | bytes 2621440 | tf_op jit(solution)/shard_map/pallas_call | solution.py:670
  31.5 2.5 %shard_map.87 = (f32[2,8,128]{2,1,0:T(8,128)}, f32[2560,128]{1,0:T(8,128)}) custom-call(f32[2,8,128]{2,1,0:T(8,128)} %get-tuple-element.8.age_any, f32[2560,128]{1,0:T(8,128)} %get-tuple-element.9.main_any, f32[3,10,8,128]{3,2,1,0:T(8,128)} %get-tuple-element.10.pack_any, f32[128,128]{1,0:T(8,128)} %get-tuple-element.11.response_any, f32[1,2]{1,0:T(1,128)} %bitcast.20), custom_call_target="tpu_custom_call" | custom-call | tf_op jit(solution)/shard_map/pallas_call | solution.py:729

commit v3 on v2

--- a/solution.py
+++ b/solution.py
@@ -422,7 +422,7 @@
         blocks = from_columns(tiles)
         for e in range(n):
             tile_send[half, e] = blocks[e]
-        exchange_start(tile_send.at[half], tile_recv.at[half], 1 + half)
+    exchange_start(tile_send.at[0], tile_recv.at[0], 1)
 
     eights = [full_dot(fourths[k], fourths[k]) for k in range(kinds)]
     e_high, e_low = two_parts(jnp.concatenate(eights, axis=0))
@@ -445,6 +445,7 @@
                 mean = main[pl.ds(2 * c, nodes, stride=stride), :]
                 value = value + (STEPS * MEAN_RATE) * mean
             main[pl.ds(2 * c + m, nodes, stride=stride), :] = value
+    exchange_start(tile_send.at[1], tile_recv.at[1], 2)
     store = pltpu.make_async_copy(main, main_any, store_sem)
     store.start()
 

time: 34.2 us -> 34 us (level)
  no operation moved by 1% of the time
where the time goes in v3:
time: 34 us; the launch traced here: 33.8 us
  Pallas kernels  33.2 us (98%)
  between operations  0.64 us (2%)
    pallas_call x1, Pallas kernels, shards(): pl.pallas_call(functools.partial(kernel, n, cap, kinds, chunks), out_shap...  30.7 us
    pallas_call x1, Pallas kernels, shards(): pl.pallas_call(functools.partial(finish, kinds, chunks), out_shape=(jax.S...  2.49 us

profile of v3, /device:TPU:0, one launch (start us, length us, event | category | flops | bytes accessed | tf_op | source)
XLA Modules:
  0.0 33.8 jit_solution(2349181977941686629)
XLA Ops:
  0.6 30.7 %shard_map.86 = (f32[2,8,128]{2,1,0:T(8,128)}, f32[2560,128]{1,0:T(8,128)}, f32[3,10,8,128]{3,2,1,0:T(8,128)}, f32[128,128]{1,0:T(8,128)}) custom-call(f32[2,8,128]{2,1,0:T(8,128)} %bitcast.16, s32[8,128]{1,0:T(8,128)} %bitcast.17, s32[8,128]{1,0:T(8,128)} %bitcast.18, f32[2560,128]{1,0:T(8,128)} %bitcast.15, f32[2,3]{1,0:T(2,128)} %vel_any.1, ...), custom_call_target="tpu_custom_call" | custom-call | flops 262144000 | bytes 2621440 | tf_op jit(solution)/shard_map/pallas_call | solution.py:671
  31.3 2.5 %shard_map.87 = (f32[2,8,128]{2,1,0:T(8,128)}, f32[2560,128]{1,0:T(8,128)}) custom-call(f32[2,8,128]{2,1,0:T(8,128)} %get-tuple-element.8.age_any, f32[2560,128]{1,0:T(8,128)} %get-tuple-element.9.main_any, f32[3,10,8,128]{3,2,1,0:T(8,128)} %get-tuple-element.10.pack_any, f32[128,128]{1,0:T(8,128)} %get-tuple-element.11.response_any, f32[1,2]{1,0:T(1,128)} %bitcast.20), custom_call_target="tpu_custom_call" | custom-call | tf_op jit(solution)/shard_map/pallas_call | solution.py:730
